TPU v7x, 256 devices: a whole 4x4x8 slice. The times are simulated.
256 devices in a mesh: resp: 16 (over y, z_hi), ctx: 16 (over x, z_lo, core).
Axes of the slice: x: 4, y: 4, z: 8 (z_hi: 4, z_lo: 2; z = z_hi * 2 + z_lo), core: 2. Of those that a mesh axis runs over, the one named last changes fastest.
Arguments:
- queries: bfloat16 [16, 2048, 2560], P('resp', 'ctx'), may hold values from -96 to 96
- resp_keys: bfloat16 [16, 2048, 512], P('resp', 'ctx'), may hold values from -6 to 6
- resp_values: bfloat16 [16, 2048, 512], P('resp', 'ctx'), may hold values from -6 to 6
- prompt_keys: bfloat16 [512, 512], P('ctx'), may hold values from -6 to 6
- prompt_values: bfloat16 [512, 512], P('ctx'), may hold values from -6 to 6
- out_grad: bfloat16 [16, 2048, 2560], P('resp', 'ctx'), may hold values from -24 to 24
- lengths: int32 [16], P('resp'), may hold values from 256 to 2048, as said below
Outputs:
- attn_out: bfloat16 [16, 2048, 2560], P('resp', 'ctx')
- query_grad: bfloat16 [16, 2048, 2560], P('resp', 'ctx')
- resp_key_grad: bfloat16 [16, 2048, 512], P('resp', 'ctx')
- resp_value_grad: bfloat16 [16, 2048, 512], P('resp', 'ctx')
- prompt_key_grad: bfloat16 [512, 512], P('ctx')
- prompt_value_grad: bfloat16 [512, 512], P('ctx')
Inputs may be any that keep to these rules, and one draw needn't show every extreme that they name: `lengths`: some response has all 2048 tokens.
All inputs are finite; a program needn't handle non-finite values.
Results may differ from a plain program's by a relative error of at most 0.023.
Values may be sent and summed in bfloat16 or wider, within the bound.
A program may use at most 128 MiB of HBM per device.

v0:
```python
import math
import jax
import jax.numpy as jnp
from jax import lax
from jax.sharding import PartitionSpec as P

DH = 128
HQ = 20
HK = 4
NEG = -1e30


def score_block(query4, keys_blk, key_pos, row_pos, scale):
    keys3 = keys_blk.reshape(keys_blk.shape[0], query4.shape[1], query4.shape[3])
    raw = jnp.einsum("nkgd,mkd->kgnm", query4, keys3, preferred_element_type=jnp.float32) * scale
    allowed = key_pos[None, :] <= row_pos[:, None]
    return jnp.where(allowed[None, None], raw, jnp.float32(NEG))


def scan_blocks(keys_all, values_all, pos_all, step, init):
    total_rows = keys_all.shape[0]
    block = math.gcd(total_rows, 512)
    count = total_rows // block
    blocks = (
        keys_all.reshape(count, block, keys_all.shape[1]),
        values_all.reshape(count, block, values_all.shape[1]),
        pos_all.reshape(count, block),
    )
    return lax.scan(step, init, blocks)


def body(queries, resp_keys, resp_values, prompt_keys, prompt_values, out_grad, lengths):
    rows = queries.shape[1]
    group = HQ // HK
    width = HK * DH
    scale = DH ** (-0.5)
    cycle = lax.axis_size("ctx")
    first_row = lax.axis_index("ctx") * rows
    row_pos = first_row + jnp.arange(rows, dtype=jnp.int32)
    row_ok = row_pos < lengths[0]
    query4 = queries[0].reshape(rows, HK, group, DH)
    grad = jnp.where(row_ok[:, None], out_grad[0], jnp.zeros_like(out_grad[0]))
    grad4 = grad.reshape(rows, HK, group, DH)
    seq_rows = resp_keys.shape[1] * cycle
    prompt_rows = prompt_keys.shape[0] * cycle

    def stats_update(stats, keys_blk, key_pos):
        top, total = stats
        scores = score_block(query4, keys_blk, key_pos, row_pos, scale)
        new_top = jnp.maximum(top, jnp.max(scores, axis=-1))
        total = total * jnp.exp(top - new_top) + jnp.sum(
            jnp.exp(scores - new_top[..., None]), axis=-1
        )
        return (new_top, total)

    top0 = jnp.full((HK, group, rows), NEG, jnp.float32)
    total0 = jnp.zeros((HK, group, rows), jnp.float32)
    pieces = (
        lax.all_gather(prompt_keys, "ctx", axis=0, tiled=True),
        lax.all_gather(prompt_values, "ctx", axis=0, tiled=True),
    )
    top = top0
    total = total0
    key_pos = jnp.full((pieces[0].shape[0],), -1, jnp.int32)
    top, total = stats_update((top, total), pieces[0], key_pos)
    key_buf = pieces[0]
    value_buf = pieces[1]
    top, total, prompt_kbuf, prompt_vbuf = (top, total, key_buf, value_buf)
    pieces = (
        lax.all_gather(resp_keys[0], "ctx", axis=0, tiled=True),
        lax.all_gather(resp_values[0], "ctx", axis=0, tiled=True),
    )
    top, total, key_buf, value_buf = (
        top,
        total,
        jnp.zeros((seq_rows, width), jnp.bfloat16),
        jnp.zeros((seq_rows, width), jnp.bfloat16),
    )
    key_pos = jnp.arange(pieces[0].shape[0], dtype=jnp.int32)
    top, total = stats_update((top, total), pieces[0], key_pos)
    key_buf = pieces[0]
    value_buf = pieces[1]
    top, total, resp_kbuf, resp_vbuf = (top, total, key_buf, value_buf)
    lse = top + jnp.log(total)
    prompt_pos = jnp.full((prompt_rows,), -1, jnp.int32)
    resp_pos = jnp.arange(seq_rows, dtype=jnp.int32)

    def out_step(acc, blk):
        keys_blk, values_blk, key_pos = blk
        scores = score_block(query4, keys_blk, key_pos, row_pos, scale)
        prob = jnp.exp(scores - lse[..., None]).astype(jnp.bfloat16)
        values3 = values_blk.reshape(values_blk.shape[0], HK, DH)
        return (
            acc + jnp.einsum("kgnm,mkd->nkgd", prob, values3, preferred_element_type=jnp.float32),
            None,
        )

    mixed0 = jnp.zeros((rows, HK, group, DH), jnp.float32)
    mixed, unused = scan_blocks(prompt_kbuf, prompt_vbuf, prompt_pos, out_step, mixed0)
    mixed, unused = scan_blocks(resp_kbuf, resp_vbuf, resp_pos, out_step, mixed)
    attn_out = jnp.where(row_ok[:, None], mixed.reshape(rows, HQ * DH), jnp.float32(0.0)).astype(
        jnp.bfloat16
    )
    delta = jnp.einsum(
        "nkgd,nkgd->kgn",
        grad4,
        attn_out.reshape(rows, HK, group, DH),
        preferred_element_type=jnp.float32,
    )

    def grads_block(keys_blk, values_blk, key_pos):
        scores = score_block(query4, keys_blk, key_pos, row_pos, scale)
        prob = jnp.exp(scores - lse[..., None])
        prob_low = prob.astype(jnp.bfloat16)
        keys3 = keys_blk.reshape(keys_blk.shape[0], HK, DH)
        values3 = values_blk.reshape(values_blk.shape[0], HK, DH)
        dprob = jnp.einsum("nkgd,mkd->kgnm", grad4, values3, preferred_element_type=jnp.float32)
        dscore = (prob * (dprob - delta[..., None])).astype(jnp.bfloat16)
        dquery = (
            jnp.einsum("kgnm,mkd->nkgd", dscore, keys3, preferred_element_type=jnp.float32) * scale
        )
        dkey = (
            jnp.einsum("kgnm,nkgd->mkd", dscore, query4, preferred_element_type=jnp.float32) * scale
        )
        dvalue = jnp.einsum("kgnm,nkgd->mkd", prob_low, grad4, preferred_element_type=jnp.float32)
        both = jnp.concatenate(
            [dkey.reshape(keys_blk.shape[0], width), dvalue.reshape(keys_blk.shape[0], width)],
            axis=1,
        )
        return (dquery, both)

    def back_step(acc, blk):
        keys_blk, values_blk, key_pos = blk
        dquery, both = grads_block(keys_blk, values_blk, key_pos)
        return (acc + dquery, both)

    dquery0 = jnp.zeros((rows, HK, group, DH), jnp.float32)
    dquery, prompt_terms = scan_blocks(prompt_kbuf, prompt_vbuf, prompt_pos, back_step, dquery0)
    prompt_term = prompt_terms.reshape(prompt_rows, 2 * width)
    dquery, resp_terms = scan_blocks(resp_kbuf, resp_vbuf, resp_pos, back_step, dquery)
    resp_sum = lax.psum_scatter(
        resp_terms.reshape(seq_rows, 2 * width), "ctx", scatter_dimension=0, tiled=True
    )
    query_grad = dquery.reshape(rows, HQ * DH).astype(jnp.bfloat16)
    prompt_part = lax.psum_scatter(prompt_term, "ctx", scatter_dimension=0, tiled=True)
    prompt_sum = lax.psum(prompt_part, "resp")
    resp_key_grad = resp_sum[:, :width].astype(jnp.bfloat16)
    resp_value_grad = resp_sum[:, width:].astype(jnp.bfloat16)
    prompt_key_grad = prompt_sum[:, :width].astype(jnp.bfloat16)
    prompt_value_grad = prompt_sum[:, width:].astype(jnp.bfloat16)
    return (
        attn_out[None],
        query_grad[None],
        resp_key_grad[None],
        resp_value_grad[None],
        prompt_key_grad,
        prompt_value_grad,
    )


def solution(mesh):
    in_specs = (
        P("resp", "ctx", None),
        P("resp", "ctx", None),
        P("resp", "ctx", None),
        P("ctx", None),
        P("ctx", None),
        P("resp", "ctx", None),
        P("resp"),
    )
    out_specs = (
        P("resp", "ctx", None),
        P("resp", "ctx", None),
        P("resp", "ctx", None),
        P("resp", "ctx", None),
        P("ctx", None),
        P("ctx", None),
    )
    return jax.shard_map(body, mesh=mesh, in_specs=in_specs, out_specs=out_specs, check_vma=False)
```

profile of v0, /device:TPU:8, one launch (start us, length us, event | category | flops | bytes accessed | tf_op | source)
XLA Modules:
  0.0 321.6 jit_solution(5401829585454170042)
XLA Ops:
  11.4 23.7 %all_gather.12 = bf16[512,512]{1,0:T(8,128)(2,1)S(1)} all-gather(bf16[32,512]{1,0:T(8,128)(2,1)} %param.14), channel_id=1, replica_groups=mesh['resp'=16,'ctx'=16] {'ctx'}, dimensions={0}, use_global_device_ids=true | all-gather | bytes 557056 | tf_op jit(solution)/shard_map/all_gather | solution.py:59
  35.3 20.1 %all_gather.14 = bf16[512,512]{1,0:T(8,128)(2,1)S(1)} all-gather(bf16[32,512]{1,0:T(8,128)(2,1)} %param.15), channel_id=1, replica_groups=mesh['resp'=16,'ctx'=16] {'ctx'}, dimensions={0}, use_global_device_ids=true | all-gather | bytes 557056 | tf_op jit(solution)/shard_map/all_gather | solution.py:60
  58.5 3.2 bitcast_reduce_fusion
  61.7 4.8 %fusion.39 = (f32[4,5,128]{2,1,0:T(8,128)S(1)}, f32[4,2048,128,5]{2,1,3,0:T(8,128)S(1)}) fusion(pred[128,2048]{0,1:T(8,128)(4,1)S(1)} %iota_compare_fusion, bf16[2048,4,128,1]{0,2,3,1:T(8,128)(2,1)} %bitcast.261, bf16[128,4,5,128]{0,3,2,1:T(8,128)(2,1)S(1)} %bitcast.245), kind=kOutput, calls=%fused_computation.49 | convolution fusion | flops 1357903360 | bytes 23996416 | tf_op jit(solution)/shard_map/nkgd,mkd->kgnm/dot_general | solution.py:15
  66.5 3.7 %fusion.43 = f32[4,5,128]{2,1,0:T(8,128)S(1)} fusion(f32[4,512,128,5]{2,1,3,0:T(8,128)} %get-tuple-element.374, f32[4,5,128]{2,1,0:T(8,128)S(1)} %get-tuple-element.371, pred[128]{0:T(512)(128)(4,1)S(1)} %broadcast_compare_fusion.2), kind=kLoop, calls=%fused_computation.56 | loop fusion | flops 5240320 | bytes 5263488 | tf_op jit(solution)/shard_map/reduce_sum | solution.py:51
  70.2 4.5 %exponential_reduce_fusion = f32[4,5,128]{2,1,0:T(8,128)S(1)} fusion(f32[4,2048,128,5]{2,1,3,0:T(8,128)S(1)} %get-tuple-element.376, f32[4,5,128]{2,1,0:T(8,128)S(1)} %get-tuple-element.372, pred[128,2048]{0,1:T(8,128)(4,1)S(1)} %iota_compare_fusion), kind=kLoop, calls=%fused_computation.48 | loop fusion | flops 20968960 | bytes 21254144 | tf_op jit(solution)/shard_map/reduce_sum | solution.py:51
  79.6 4.5 %reshape.290 = bf16[4,512,512]{1,0,2:T(4,128)(2,1)} reshape(bf16[1,2048,512]{1,2,0:T(8,128)(2,1)} %all-gather.5.cloned.1.call-done) | data formatting | bytes 4194304 | tf_op jit(solution)/shard_map/reshape | solution.py:25
  84.1 3.3 %copy.171 = bf16[4,512,512]{1,2,0:T(8,128)(2,1)} copy(bf16[4,512,512]{1,0,2:T(4,128)(2,1)} %reshape.290) | data formatting | bytes 4194304
  87.5 6.5 %all-gather.7.cloned.1.call-done = bf16[1,2048,512]{2,1,0:T(8,128)(2,1)} async-done(((bf16[1,128,512]{2,1,0:T(8,128)(2,1)}), bf16[1,2048,512]{2,1,0:T(8,128)(2,1)}) %all-gather.7.cloned.1.call-update) | async-done | bytes 2097168 | tf_op jit(solution)/shard_map/all_gather | solution.py:71
  93.9 4.1 %copy.170 = bf16[4,512,512]{1,2,0:T(8,128)(2,1)} copy(bf16[4,512,512]{2,1,0:T(8,128)(2,1)} %bitcast.267) | data formatting | bytes 4194304
  98.1 21.0 %while.6 = (s32[]{:T(128)}, f32[128,4,5,128]{0,3,2,1:T(8,128)S(1)}, bf16[4,512,512]{1,2,0:T(8,128)(2,1)}, s32[4,512]{1,0:T(4,128)S(1)}, bf16[4,512,512]{1,2,0:T(...) while((s32[]{:T(128)}, ...), condition=%wide.region_5.6_spmd.clone, body=%wide.region_4.5_spmd.clone.sunk | while | flops 676724864 | bytes 6571113 | solution.py:29
  100.1 3.1 fusion.108
  105.3 3.1 fusion.108
  110.6 3.1 fusion.108
  115.8 3.1 fusion.108
  121.1 5.3 %fusion.50 = f32[4,128,512,1]{2,1,3,0:T(8,128)} fusion(bf16[128,4,5,128]{0,3,2,1:T(8,128)(2,1)S(1)} %get-tuple-element.536, f32[4,512,128,5]{2,1,3,0:T(8,128)} %get-tuple-element.374, f32[4,5,128]{2,1,0:T(8,128)} %get-tuple-element.581, pred[128]{0:T(512)(128)(4,1)S(1)} %broadcast_compare_fusion.3), kind=kOutput, calls=%fused_computation.75 | convolution fusion | flops 340787200 | bytes 6957184 | tf_op jit(solution)/shard_map/while/body/eval_jaxpr/kgnm,nkgd->mkd/dot_general | solution.py:125
  133.9 3.1 pad_maximum_fusion
  138.6 69.7 %while.7 = (s32[]{:T(128)}, f32[128,4,5,128]{0,3,2,1:T(8,128)}, f32[4,512,1024]{2,1,0:T(8,128)}, bf16[4,512,512]{1,2,0:T(8,128)(2,1)}, s32[4,512]{1,0:T(4,128)S(...) while((s32[]{:T(128)}, f32[128,4,5,128]{0,3,2,1:T(8,128)}, ...), condition=%wide.region_7.8_spmd.clone, body=%wide.region_6.7_spmd.clone.sunk | while | flops 1692336256 | bytes 52139704 | solution.py:29
  146.7 2.9 copy.245
  149.6 3.2 constant_dynamic-update-slice_fusion.2
  152.8 3.2 fusion.121
  164.1 2.9 copy.245
  167.0 3.2 constant_dynamic-update-slice_fusion.2
  170.2 3.2 fusion.121
  181.5 2.9 copy.245
  184.4 3.2 constant_dynamic-update-slice_fusion.2
  187.6 3.2 fusion.121
  198.9 2.9 copy.245
  201.8 3.2 constant_dynamic-update-slice_fusion.2
  205.0 3.2 fusion.121
  211.9 81.9 %all-reduce.1 = bf16[32,1024]{1,0:T(8,128)(2,1)S(1)} all-reduce(f32[32,1024]{1,0:T(8,128)} %reduce-scatter.5.cloned.1.call-done), channel_id=1, replica_groups=mesh['resp'=16,'ctx'=16] {'resp'}, use_global_device_ids=true, to_apply=%region_10.11 | all-reduce | flops 32768 | bytes 196608 | tf_op jit(solution)/shard_map/psum | solution.py:146
  294.5 18.8 %reduce-scatter.3.cloned.1.call-done = f32[128,1024]{1,0:T(8,128)} async-done(((f32[2048,1024]{1,0:T(8,128)}), f32[128,1024]{1,0:T(8,128)}) %reduce-scatter.3.cloned.1.call-update) | async-done | bytes 524304 | tf_op jit(solution)/shard_map/reduce_scatter | solution.py:141
  (143 shorter events, 69.0 us)
Async XLA Ops:
  7.2 50.2 %copy-start.4 = (bf16[1,128,2560]{2,1,0:T(8,128)(2,1)S(1)}, bf16[1,128,2560]{2,1,0:T(8,128)(2,1)}, u32[]{:S(2)}) copy-start(bf16[1,128,2560]{2,1,0:T(8,128)(2,1)} %param.16) | copy-start | bytes 1966084
  7.2 54.5 %all-gather.5.cloned.1.call-start = ((), (), s32[]{:S(2)}) async-start(), calls=%async_computation.4 | async-start | bytes 2228224 | tf_op jit(solution)/shard_map/all_gather | solution.py:70
  9.0 85.0 %all-gather.7.cloned.1.call-start = ((), (), s32[]{:S(2)}) async-start(), calls=%async_computation.5 | async-start | bytes 2228224 | tf_op jit(solution)/shard_map/all_gather | solution.py:71
  9.7 202.2 %reduce-scatter.5.cloned.1.call-start = ((), (), s32[]{:S(2)}) async-start(), calls=%async_computation.3 | async-start | bytes 2228224 | tf_op jit(solution)/shard_map/reduce_scatter | solution.py:145
  55.6 19.1 %copy-start.7 = (bf16[512,512]{0,1:T(8,128)(2,1)}, bf16[512,512]{0,1:T(8,128)(2,1)S(1)}, u32[]{:S(2)}) copy-start(bf16[512,512]{0,1:T(8,128)(2,1)S(1)} %copy.166) | copy-start | bytes 1572868
  66.5 8.9 %slice-start = ((s8[5242880]{0:T(1024)(128)(4,1)}), s8[4194304]{0:T(1024)(128)(4,1)S(1)}, s32[]{:S(2)}) async-start(s8[5242880]{0:T(1024)(128)(4,1)} %bitcast.252), calls=%async_computation.6 | async-start | bytes 8388608
  70.2 5.2 %slice-start.1 = ((s8[5242880]{0:T(1024)(128)(4,1)}), s8[1048576]{0:T(1024)(128)(4,1)S(1)}, s32[]{:S(2)}) async-start(s8[5242880]{0:T(1024)(128)(4,1)} %bitcast.252), calls=%async_computation.7 | async-start | bytes 2097152
  74.8 0.6 copy-start.11
  119.1 7.2 %copy-start.2 = (f32[128,4,5,128]{0,3,2,1:T(8,128)}, f32[128,4,5,128]{0,3,2,1:T(8,128)S(1)}, u32[]{:S(2)}) copy-start(f32[128,4,5,128]{0,3,2,1:T(8,128)S(1)} %get-tuple-element.157) | copy-start | bytes 3932164
  119.1 7.2 %slice-start.2 = ((s8[5242880]{0:T(1024)(128)(4,1)}), s8[4194304]{0:T(1024)(128)(4,1)S(1)}, s32[]{:S(2)}) async-start(s8[5242880]{0:T(1024)(128)(4,1)} %bitcast.254), calls=%async_computation.8 | async-start | bytes 8388608
  119.1 7.2 %copy-start.8 = (bf16[512,512]{0,1:T(8,128)(2,1)S(1)}, bf16[512,512]{0,1:T(8,128)(2,1)}, u32[]{:S(2)}) copy-start(bf16[512,512]{0,1:T(8,128)(2,1)} %copy-done.7) | copy-start | bytes 1572868
  119.1 7.2 %copy-start.12 = (f32[4,5,128]{2,1,0:T(8,128)S(1)}, f32[4,5,128]{2,1,0:T(8,128)}, u32[]{:S(2)}) copy-start(f32[4,5,128]{2,1,0:T(8,128)} %get-tuple-element.581) | copy-start | bytes 30724
  121.0 7.0 %copy-start.5 = (bf16[128,4,5,128]{0,3,2,1:T(8,128)(2,1)}, bf16[128,4,5,128]{0,3,2,1:T(8,128)(2,1)S(1)}, u32[]{:S(2)}) copy-start(bf16[128,4,5,128]{0,3,2,1:T(8,128)(2,1)S(1)} %get-tuple-element.536) | copy-start | bytes 1966084
  121.0 7.0 %copy-start.9 = (f32[4,5,128]{2,1,0:T(8,128)}, f32[4,5,128]{2,1,0:T(8,128)S(1)}, u32[]{:S(2)}) copy-start(f32[4,5,128]{2,1,0:T(8,128)S(1)} %get-tuple-element.537) | copy-start | bytes 30724
  121.1 5.3 %slice-start.3 = ((s8[5242880]{0:T(1024)(128)(4,1)}), s8[1048576]{0:T(1024)(128)(4,1)S(1)}, s32[]{:S(2)}) async-start(s8[5242880]{0:T(1024)(128)(4,1)} %bitcast.254), calls=%async_computation.9 | async-start | bytes 2097152
  132.6 5.9 %copy-start.10 = (f32[4,5,128]{2,1,0:T(8,128)S(1)}, f32[4,5,128]{2,1,0:T(8,128)}, u32[]{:S(2)}) copy-start(f32[4,5,128]{2,1,0:T(8,128)} %copy-done.9) | copy-start | bytes 30724
  132.6 5.9 %copy-start.13 = (f32[4,5,128]{2,1,0:T(8,128)S(1)}, f32[4,5,128]{2,1,0:T(8,128)}, u32[]{:S(2)}) copy-start(f32[4,5,128]{2,1,0:T(8,128)} %get-tuple-element.581) | copy-start | bytes 30724
  137.0 176.3 %reduce-scatter.3.cloned.1.call-start = ((), (), s32[]{:S(2)}) async-start(), calls=%async_computation.2 | async-start | bytes 8912896 | tf_op jit(solution)/shard_map/reduce_scatter | solution.py:141
  138.6 2.4 copy-start.6
  139.9 1.1 copy-start
  156.0 2.4 copy-start.6
  157.3 1.1 copy-start
  173.4 2.4 copy-start.6
  174.7 1.1 copy-start
  190.8 2.4 copy-start.6
  192.1 1.1 copy-start
  208.2 1.3 copy-start.1
  208.2 2.5 copy-start.3
Sparse Core Ops, SparseCore 0:
  10.4 43.8 all-gather.4
  56.1 37.7 all-gather.6
  137.1 66.8 reduce-scatter.4
  208.4 104.8 reduce-scatter.2
where the time goes:
time: 323 us; the launch traced here: 322 us
  blocking collectives  126 us (39%)
  local copies, waits for them, and re-layouts  65.2 us (20%)
  matrix products  64.7 us (20%)
  waiting for transfers between devices  26 us (8%)
  other arithmetic  24.4 us (8%)
  between operations  14.7 us (5%)
    psum x1, blocking collectives, body(): prompt_sum = lax.psum(prompt_part, 'resp')  81.9 us
    dynamic_update_slice x8, local copies, waits for them, and re-layouts, scan_blocks(): return lax.scan(step, init, blocks)  24.5 us
    all_gather x1, blocking collectives, body(): lax.all_gather(prompt_keys, 'ctx', axis=0, tiled=True)  23.7 us
    all_gather x1, blocking collectives, body(): lax.all_gather(prompt_values, 'ctx', axis=0, tiled=True)  20.1 us
    unnamed x42, local copies, waits for them, and re-layouts  20 us
    reduce_scatter x1, waiting for transfers between devices, body(): lax.psum_scatter(resp_terms.reshape(seq_rows, 2 * width), 'ctx', scatter_...  18.8 us
    dot_general x5, matrix products, out_step(): jnp.einsum('kgnm,mkd->nkgd', prob, values3, preferred_element_type=jnp.fl...  15.1 us
    dot_general x5, matrix products, grads_block(): jnp.einsum('kgnm,mkd->nkgd', dscore, keys3, preferred_element_type=jnp.fl...  13.8 us
  transfers between devices with their start and end apart: 4, of which 2 were waited for; matrix products, arithmetic and copies ran while one was open for 33% of the time, Pallas kernels for 0%

commit v1 on v0

--- a/solution.py
+++ b/solution.py
@@ -143,7 +143,7 @@
     )
     query_grad = dquery.reshape(rows, HQ * DH).astype(jnp.bfloat16)
     prompt_part = lax.psum_scatter(prompt_term, "ctx", scatter_dimension=0, tiled=True)
-    prompt_sum = lax.psum(prompt_part, "resp")
+    prompt_sum = jnp.sum(lax.all_gather(prompt_part, "resp"), axis=0)
     resp_key_grad = resp_sum[:, :width].astype(jnp.bfloat16)
     resp_value_grad = resp_sum[:, width:].astype(jnp.bfloat16)
     prompt_key_grad = prompt_sum[:, :width].astype(jnp.bfloat16)

time: 323 us -> 382 us (1.18)
  waiting for transfers between devices: 26 us -> 161 us
  blocking collectives: 126 us -> 43.8 us
  matrix products: 64.7 us -> 69.5 us
    psum x1 -> x0, blocking collectives: 81.9 us -> none  [body(): prompt_sum = lax.psum(prompt_part, 'resp')]
    reduce_scatter x1, waiting for transfers between devices: 18.8 us -> 92.6 us  [body(): lax.psum_scatter(resp_terms.reshape(seq_rows, 2 * width), 'ctx', scatter_...]
    reduce_scatter x1, waiting for transfers between devices: 0.01 us -> 60.9 us  [body(): lax.psum_scatter(prompt_term, 'ctx', scatter_dimension=0, tiled=True)]
    unnamed x42 -> x28, local copies, waits for them, and re-layouts: 20 us -> 21.6 us
  transfers between devices with their start and end apart: 4 -> 5, of which waited for: 2 -> 3; matrix products, arithmetic and copies ran while one was open for 33% -> 30% of each run, Pallas kernels for 0% -> 0%
where the time goes in v1:
time: 382 us; the launch traced here: 380 us
  waiting for transfers between devices  161 us (42%)
  matrix products  69.5 us (18%)
  local copies, waits for them, and re-layouts  66.7 us (17%)
  blocking collectives  43.8 us (11%)
  other arithmetic  23.5 us (6%)
  between operations  14.7 us (4%)
    reduce_scatter x1, waiting for transfers between devices, body(): lax.psum_scatter(resp_terms.reshape(seq_rows, 2 * width), 'ctx', scatter_...  92.6 us
    reduce_scatter x1, waiting for transfers between devices, body(): lax.psum_scatter(prompt_term, 'ctx', scatter_dimension=0, tiled=True)  60.9 us
    dynamic_update_slice x8, local copies, waits for them, and re-layouts, scan_blocks(): return lax.scan(step, init, blocks)  24.3 us
    all_gather x1, blocking collectives, body(): lax.all_gather(prompt_keys, 'ctx', axis=0, tiled=True)  23.7 us
    unnamed x28, local copies, waits for them, and re-layouts  21.6 us
    all_gather x1, blocking collectives, body(): lax.all_gather(prompt_values, 'ctx', axis=0, tiled=True)  20.1 us
    dot_general x5, matrix products, grads_block(): jnp.einsum('kgnm,mkd->nkgd', dscore, keys3, preferred_element_type=jnp.fl...  16 us
    dot_general x5, matrix products, out_step(): jnp.einsum('kgnm,mkd->nkgd', prob, values3, preferred_element_type=jnp.fl...  15.1 us
  transfers between devices with their start and end apart: 5, of which 3 were waited for; matrix products, arithmetic and copies ran while one was open for 30% of the time, Pallas kernels for 0%

profile of v1, /device:TPU:8, one launch (start us, length us, event | category | flops | bytes accessed | tf_op | source)
XLA Modules:
  0.0 380.5 jit_solution(5974117597414365941)
XLA Ops:
  11.4 23.7 %all_gather.18 = bf16[512,512]{1,0:T(8,128)(2,1)S(1)} all-gather(bf16[32,512]{1,0:T(8,128)(2,1)} %param.14), channel_id=1, replica_groups=mesh['resp'=16,'ctx'=16] {'ctx'}, dimensions={0}, use_global_device_ids=true | all-gather | bytes 557056 | tf_op jit(solution)/shard_map/all_gather | solution.py:59
  35.3 20.1 %all_gather.20 = bf16[512,512]{1,0:T(8,128)(2,1)S(1)} all-gather(bf16[32,512]{1,0:T(8,128)(2,1)} %param.15), channel_id=1, replica_groups=mesh['resp'=16,'ctx'=16] {'ctx'}, dimensions={0}, use_global_device_ids=true | all-gather | bytes 557056 | tf_op jit(solution)/shard_map/all_gather | solution.py:60
  58.5 3.2 bitcast_reduce_fusion
  61.7 4.8 %fusion.39 = (f32[4,5,128]{2,1,0:T(8,128)S(1)}, f32[4,2048,128,5]{2,1,3,0:T(8,128)S(1)}) fusion(pred[128,2048]{0,1:T(8,128)(4,1)S(1)} %iota_compare_fusion, bf16[2048,4,128,1]{0,2,3,1:T(8,128)(2,1)} %bitcast.260, bf16[128,4,5,128]{0,3,2,1:T(8,128)(2,1)S(1)} %bitcast.246), kind=kOutput, calls=%fused_computation.49 | convolution fusion | flops 1357903360 | bytes 23996416 | tf_op jit(solution)/shard_map/nkgd,mkd->kgnm/dot_general | solution.py:15
  66.5 3.7 fusion.43
  70.2 4.5 %exponential_reduce_fusion = f32[4,5,128]{2,1,0:T(8,128)S(1)} fusion(f32[4,2048,128,5]{2,1,3,0:T(8,128)S(1)} %get-tuple-element.376, f32[4,5,128]{2,1,0:T(8,128)S(1)} %get-tuple-element.372, pred[128,2048]{0,1:T(8,128)(4,1)S(1)} %iota_compare_fusion), kind=kLoop, calls=%fused_computation.48 | loop fusion | flops 20968960 | bytes 21254144 | tf_op jit(solution)/shard_map/reduce_sum | solution.py:51
  79.1 4.5 %reshape.290 = bf16[4,512,512]{1,0,2:T(4,128)(2,1)} reshape(bf16[1,2048,512]{1,2,0:T(8,128)(2,1)} %all-gather.7.cloned.1.call-done) | data formatting | bytes 4194304 | tf_op jit(solution)/shard_map/reshape | solution.py:25
  83.6 3.4 copy.169
  87.0 6.9 %all-gather.9.cloned.1.call-done = bf16[1,2048,512]{2,1,0:T(8,128)(2,1)} async-done(((bf16[1,128,512]{2,1,0:T(8,128)(2,1)}), bf16[1,2048,512]{2,1,0:T(8,128)(2,1)}) %all-gather.9.cloned.1.call-update) | async-done | bytes 2097168 | tf_op jit(solution)/shard_map/all_gather | solution.py:71
  93.9 4.1 %copy.168 = bf16[4,512,512]{1,2,0:T(8,128)(2,1)} copy(bf16[4,512,512]{2,1,0:T(8,128)(2,1)} %bitcast.267) | data formatting | bytes 4194304
  98.0 18.5 %while.6 = (s32[]{:T(128)}, f32[128,4,5,128]{0,3,2,1:T(8,128)S(1)}, bf16[4,512,512]{1,2,0:T(8,128)(2,1)}, s32[4,512]{1,0:T(4,128)S(1)}, bf16[4,512,512]{1,2,0:T(...) while((s32[]{:T(128)}, ...), condition=%wide.region_5.6_spmd.clone, body=%wide.region_4.5_spmd.clone.sunk | while | flops 676724864 | bytes 6571113 | solution.py:29
  99.5 3.1 fusion.108
  104.1 3.1 fusion.108
  108.6 3.1 fusion.108
  113.2 3.1 fusion.108
  119.3 3.8 %fusion.50 = f32[4,128,512,1]{2,1,3,0:T(8,128)S(1)} fusion(bf16[128,4,5,128]{0,3,2,1:T(8,128)(2,1)S(1)} %get-tuple-element.536, f32[4,512,128,5]{2,1,3,0:T(8,128)} %get-tuple-element.374, f32[4,5,128]{2,1,0:T(8,128)S(1)} %get-tuple-element.585, pred[128]{0:T(512)(128)(4,1)S(1)} %broadcast_compare_fusion.3), kind=kOutput, calls=%fused_computation.75 | convolution fusion | flops 340787200 | bytes 6957184 | tf_op jit(solution)/shard_map/while/body/eval_jaxpr/kgnm,nkgd->mkd/dot_general | solution.py:125
  124.5 4.5 %fusion.41 = bf16[4,5,128,512]{2,3,1,0:T(8,128)(2,1)S(1)} fusion(f32[4,512,128,5]{2,1,3,0:T(8,128)} %get-tuple-element.374, f32[4,5,128]{2,1,0:T(8,128)S(1)} %get-tuple-element.537, f32[4,5,128]{2,1,0:T(8,128)S(1)} %get-tuple-element.585, pred[128]{0:T(512)(128)(4,1)S(1)} %broadcast_compare_fusion.3, bf16[128,4,5,128]{0,3,2,1:T(8,128)(2,1)} %copy-done.6, ...), kind=kOutput, calls=%fused_computation.52 | convolution fusion | flops 343408640 | bytes 9064576 | tf_op jit(solution)/shard_map/while/body/eval_jaxpr/nkgd,mkd->kgnm/dot_general | solution.py:117
  133.6 3.1 pad_maximum_fusion
  136.7 3.2 fusion.46
  142.7 60.9 %reduce-scatter.5.cloned.1.call-done = f32[32,1024]{1,0:T(8,128)} async-done(((f32[512,1024]{1,0:T(8,128)}), f32[32,1024]{1,0:T(8,128)}) %reduce-scatter.5.cloned.1.call-update) | async-done | bytes 131088 | tf_op jit(solution)/shard_map/reduce_scatter | solution.py:145
  203.7 69.7 %while.7 = (s32[]{:T(128)}, f32[128,4,5,128]{0,3,2,1:T(8,128)}, f32[4,512,1024]{2,1,0:T(8,128)}, bf16[4,512,512]{1,2,0:T(8,128)(2,1)}, s32[4,512]{1,0:T(4,128)S(...) while((s32[]{:T(128)}, f32[128,4,5,128]{0,3,2,1:T(8,128)}, ...), condition=%wide.region_7.8_spmd.clone, body=%wide.region_6.7_spmd.clone.sunk | while | flops 1692336256 | bytes 52139704 | solution.py:29
  212.1 2.9 copy.244
  214.9 3.2 constant_dynamic-update-slice_fusion.2
  218.2 3.2 fusion.121
  229.4 2.9 copy.244
  232.3 3.2 constant_dynamic-update-slice_fusion.2
  235.5 3.2 fusion.121
  249.6 3.2 constant_dynamic-update-slice_fusion.2
  252.9 3.2 fusion.121
  267.1 3.2 constant_dynamic-update-slice_fusion.2
  270.3 3.2 fusion.121
  279.5 92.6 %reduce-scatter.3.cloned.1.call-done = f32[128,1024]{1,0:T(8,128)} async-done(((f32[2048,1024]{1,0:T(8,128)}), f32[128,1024]{1,0:T(8,128)}) %reduce-scatter.3.cloned.1.call-update) | async-done | bytes 524304 | tf_op jit(solution)/shard_map/reduce_scatter | solution.py:141
  (131 shorter events, 74.0 us)
Async XLA Ops:
  7.2 50.2 %copy-start.5 = (bf16[1,128,2560]{2,1,0:T(8,128)(2,1)S(1)}, bf16[1,128,2560]{2,1,0:T(8,128)(2,1)}, u32[]{:S(2)}) copy-start(bf16[1,128,2560]{2,1,0:T(8,128)(2,1)} %param.16) | copy-start | bytes 1966084
  7.2 54.5 %all-gather.7.cloned.1.call-start = ((), (), s32[]{:S(2)}) async-start(), calls=%async_computation.4 | async-start | bytes 2228224 | tf_op jit(solution)/shard_map/all_gather | solution.py:70
  9.0 84.9 %all-gather.9.cloned.1.call-start = ((), (), s32[]{:S(2)}) async-start(), calls=%async_computation.5 | async-start | bytes 2228224 | tf_op jit(solution)/shard_map/all_gather | solution.py:71
  9.7 193.9 %reduce-scatter.5.cloned.1.call-start = ((), (), s32[]{:S(2)}) async-start(), calls=%async_computation.3 | async-start | bytes 2228224 | tf_op jit(solution)/shard_map/reduce_scatter | solution.py:145
  35.3 26.4 %copy-start.4 = (bf16[512,512]{0,1:T(8,128)(2,1)}, bf16[512,512]{0,1:T(8,128)(2,1)S(1)}, u32[]{:S(2)}) copy-start(bf16[512,512]{0,1:T(8,128)(2,1)S(1)} %copy.157) | copy-start | bytes 1572868
  55.6 19.1 %copy-start.8 = (bf16[512,512]{0,1:T(8,128)(2,1)}, bf16[512,512]{0,1:T(8,128)(2,1)S(1)}, u32[]{:S(2)}) copy-start(bf16[512,512]{0,1:T(8,128)(2,1)S(1)} %copy.164) | copy-start | bytes 1572868
  66.5 8.3 %slice-start = ((s8[5242880]{0:T(1024)(128)(4,1)}), s8[4194304]{0:T(1024)(128)(4,1)S(1)}, s32[]{:S(2)}) async-start(s8[5242880]{0:T(1024)(128)(4,1)} %bitcast.253), calls=%async_computation.7 | async-start | bytes 8388608
  70.2 4.6 %slice-start.1 = ((s8[5242880]{0:T(1024)(128)(4,1)}), s8[1048576]{0:T(1024)(128)(4,1)S(1)}, s32[]{:S(2)}) async-start(s8[5242880]{0:T(1024)(128)(4,1)} %bitcast.253), calls=%async_computation.8 | async-start | bytes 2097152
  116.6 6.5 %copy-start.2 = (f32[128,4,5,128]{0,3,2,1:T(8,128)}, f32[128,4,5,128]{0,3,2,1:T(8,128)S(1)}, u32[]{:S(2)}) copy-start(f32[128,4,5,128]{0,3,2,1:T(8,128)S(1)} %get-tuple-element.157) | copy-start | bytes 3932164
  118.4 0.8 copy-start.6
  136.7 140.5 %all-gather.11.cloned.1.call-start = ((), (), s32[]{:S(2)}) async-start(), calls=%async_computation.6 | async-start | bytes 2228224 | tf_op jit(solution)/shard_map/all_gather | solution.py:146
  203.7 168.5 %reduce-scatter.3.cloned.1.call-start = ((), (), s32[]{:S(2)}) async-start(), calls=%async_computation.2 | async-start | bytes 8912896 | tf_op jit(solution)/shard_map/reduce_scatter | solution.py:141
  203.9 2.4 copy-start.7
  205.3 1.1 copy-start
  221.3 2.4 copy-start.7
  222.7 1.1 copy-start
  238.7 2.4 copy-start.7
  240.0 1.1 copy-start
  256.1 2.4 copy-start.7
  257.4 1.1 copy-start
  273.4 1.3 copy-start.1
  273.5 2.5 copy-start.3
Sparse Core Ops, SparseCore 0:
  10.4 43.9 all-gather.6
  56.2 37.6 all-gather.8
  136.8 66.8 reduce-scatter.4
  205.9 57.2 all-gather.10
  273.6 98.4 reduce-scatter.2
